TPU v7x, 128 devices: a whole 4x4x4 slice. The times are simulated.
128 devices in a mesh: bucket: 32 (over z, x_lo, y), seq: 4 (over x_hi, core).
Axes of the slice: x: 4 (x_hi: 2, x_lo: 2; x = x_hi * 2 + x_lo), y: 4, z: 4, core: 2. Of those that a mesh axis runs over, the one named last changes fastest.
Arguments:
- tokens: bfloat16 [32, 1024, 1024], P('bucket', 'seq'), may hold values from -6 to 6
- condition: bfloat16 [32, 1024], P('bucket'), may hold values from -6 to 6
- lengths: int32 [32, 2], P('bucket'), may hold values from 64 to 896, as said below
- head_mask: int32 [32, 16], P('bucket'), may hold values 0 or 1
- group_mask: int32 [32, 16], P('bucket'), may hold values 0 or 1
- token_mask: int32 [32, 1024], P('bucket', 'seq'), may hold values 0 or 1
- ada_weight: bfloat16 [1024, 6144], replicated, may hold values from -0.1875 to 0.1875
- ada_bias: bfloat16 [6144], replicated, may hold values from -3 to 3
- qkv_weight: bfloat16 [1024, 3072], replicated, may hold values from -0.1875 to 0.1875
- qv_bias: bfloat16 [2048], replicated, may hold values from -3 to 3
- proj_weight: bfloat16 [1024, 1024], replicated, may hold values from -0.75 to 0.75
- proj_bias: bfloat16 [1024], replicated, may hold values from -3 to 3
- fc1_weight: bfloat16 [1024, 4096], replicated, may hold values from -0.1875 to 0.1875
- fc1_bias: bfloat16 [4096], replicated, may hold values from -3 to 3
- fc2_weight: bfloat16 [4096, 1024], replicated, may hold values from -0.09375 to 0.09375
- fc2_bias: bfloat16 [1024], replicated, may hold values from -3 to 3
- out_grad: bfloat16 [32, 1024, 1024], P('bucket', 'seq'), may hold values from -6 to 6
Outputs:
- block_out: float32 [32, 1024, 1024], P('bucket', 'seq')
- input_grad: float32 [32, 1024, 1024], P('bucket', 'seq')
- cond_grad: float32 [32, 1024], P('bucket')
- ada_weight_grad: float32 [1024, 6144], P('bucket')
- ada_bias_grad: float32 [6144], P('bucket')
- qkv_weight_grad: float32 [1024, 3072], P('bucket')
- qv_bias_grad: float32 [2048], P('bucket')
- proj_weight_grad: float32 [1024, 1024], P('bucket')
- proj_bias_grad: float32 [1024], P('bucket')
- fc1_weight_grad: float32 [1024, 4096], P('bucket')
- fc1_bias_grad: float32 [4096], P('bucket')
- fc2_weight_grad: float32 [4096, 1024], P('bucket')
- fc2_bias_grad: float32 [1024], P('bucket')
Inputs may be any that keep to these rules, and one draw needn't show every extreme that they name: `lengths`: lengths of a bucket's two items in the order in which they lie in its row from position 0; they sum to 960, so the last 64 positions of every row are padding.
All inputs are finite; a program needn't handle non-finite values. No bound on the sum of `head_mask` or of `group_mask` or of `token_mask` on one device may be relied on, other than what follows from the above.
Results may differ from a plain program's by a relative error of at most 0.025.
Values may be sent and summed in bfloat16 or wider, within the bound.
A program may use at most 256 MiB of HBM per device.

v0:
```python
import jax
import jax.numpy as jnp
from jax import lax
from jax.sharding import PartitionSpec as P


def normalize(values):
    centred = values - jnp.mean(values, axis=-1, keepdims=True)
    return centred * lax.rsqrt(jnp.mean(centred * centred, axis=-1, keepdims=True) + 1e-06)


def gelu_tanh(values):
    return (
        0.5
        * values
        * (1.0 + jnp.tanh(0.7978845608028654 * (values + 0.044715 * values * values * values)))
    )


def product(first_op, second_op):
    return jnp.dot(first_op, second_op, preferred_element_type=jnp.float32)


def over_rows(first_op, second_op):
    return lax.dot_general(
        first_op, second_op, (((0,), (0,)), ((), ())), preferred_element_type=jnp.float32
    )


def against(first_op, second_op):
    return lax.dot_general(
        first_op, second_op, (((1,), (1,)), ((), ())), preferred_element_type=jnp.float32
    )


def segment_ids(positions, first_end, both_end):
    return (positions >= first_end).astype(jnp.int32) + (positions >= both_end).astype(jnp.int32)


def masked_scores(query_heads, key_heads, allowed, score_scale):
    raw_scores = jnp.einsum(
        "qhd,khd->hqk", query_heads, key_heads, preferred_element_type=jnp.float32
    )
    return jnp.where(allowed[None], raw_scores * score_scale, -1e30)


def local(
    tokens,
    condition,
    lengths,
    head_mask,
    group_mask,
    token_mask,
    ada_weight,
    ada_bias,
    qkv_weight,
    qv_bias,
    proj_weight,
    proj_bias,
    fc1_weight,
    fc1_bias,
    fc2_weight,
    fc2_bias,
    out_grad,
):
    model_width = tokens.shape[2]
    local_rows = tokens.shape[1]
    full_rows = local_rows * lax.axis_size("seq")
    heads_count = head_mask.shape[1]
    head_width = model_width // heads_count
    score_scale = head_width ** (-0.5)
    row_start = lax.axis_index("seq") * local_rows
    local_pos = row_start + jnp.arange(local_rows, dtype=jnp.int32)
    all_pos = jnp.arange(full_rows, dtype=jnp.int32)
    first_end = lengths[0, 0]
    both_end = lengths[0, 0] + lengths[0, 1]
    allowed = (
        segment_ids(local_pos, first_end, both_end)[:, None]
        == segment_ids(all_pos, first_end, both_end)[None, :]
    )
    valid_rows = (local_pos < both_end).astype(jnp.float32)[:, None]
    kept_rows = valid_rows * token_mask[0].astype(jnp.float32)[:, None]
    head_keep = head_mask[0].astype(jnp.bfloat16)[None, :, None]
    channel_mask = jnp.repeat(
        group_mask[0].astype(jnp.float32), fc1_weight.shape[1] // group_mask.shape[1]
    )
    inputs = tokens[0].astype(jnp.float32)
    upstream = out_grad[0].astype(jnp.float32)
    silu_value, silu_back = jax.vjp(jax.nn.silu, condition[0].astype(jnp.float32))
    silu_low = silu_value.astype(jnp.bfloat16)
    modulation = product(silu_low[None, :], ada_weight)[0] + ada_bias.astype(jnp.float32)
    shift_one, scale_one, gate_one, shift_two, scale_two, gate_two = jnp.split(modulation, 6)
    normed_one, norm_back_one = jax.vjp(normalize, inputs)
    normed = (normed_one * (1.0 + scale_one) + shift_one).astype(jnp.bfloat16)
    projected = product(normed, qkv_weight)
    bias_values = qv_bias.astype(jnp.float32)
    queries = (projected[:, :model_width] + bias_values[:model_width]).astype(jnp.bfloat16)
    key_rows = projected[:, model_width : 2 * model_width].astype(jnp.bfloat16)
    value_rows = (projected[:, 2 * model_width :] + bias_values[model_width:]).astype(jnp.bfloat16)
    key_all, value_all = (
        lax.all_gather(key_rows, "seq", axis=0, tiled=True),
        lax.all_gather(value_rows, "seq", axis=0, tiled=True),
    )
    query_heads = queries.reshape(local_rows, heads_count, head_width)
    key_heads = key_all.reshape(full_rows, heads_count, head_width)
    value_heads = value_all.reshape(full_rows, heads_count, head_width)
    scores = masked_scores(query_heads, key_heads, allowed, score_scale)
    largest = jnp.max(scores, axis=-1, keepdims=True)
    log_total = largest + jnp.log(jnp.sum(jnp.exp(scores - largest), axis=-1, keepdims=True))
    probs_low = jnp.exp(scores - log_total).astype(jnp.bfloat16)
    context = jnp.einsum("hqk,khd->qhd", probs_low, value_heads, preferred_element_type=jnp.float32)
    attended = (context * head_keep).reshape(local_rows, model_width).astype(jnp.bfloat16)
    branch = product(attended, proj_weight) + proj_bias.astype(jnp.float32)
    middle = inputs + valid_rows * gate_one * branch
    normed_mid, norm_back_two = jax.vjp(normalize, middle)
    normed_two = (normed_mid * (1.0 + scale_two) + shift_two).astype(jnp.bfloat16)
    hidden = product(normed_two, fc1_weight) + fc1_bias.astype(jnp.float32)
    gelu_value, gelu_back = jax.vjp(gelu_tanh, hidden)
    activated = (gelu_value * channel_mask).astype(jnp.bfloat16)
    mlp_out = product(activated, fc2_weight) + fc2_bias.astype(jnp.float32)
    block_out = middle + kept_rows * gate_two * mlp_out
    mlp_grad = (kept_rows * gate_two * upstream).astype(jnp.bfloat16)
    gate_two_grad = jnp.sum(kept_rows * mlp_out * upstream, axis=0)
    fc2_w_grad = over_rows(activated, mlp_grad)
    fc2_b_grad = jnp.sum(mlp_grad.astype(jnp.float32), axis=0)
    hidden_grad = gelu_back(against(mlp_grad, fc2_weight) * channel_mask)[0].astype(jnp.bfloat16)
    fc1_w_grad = over_rows(normed_two, hidden_grad)
    fc1_b_grad = jnp.sum(hidden_grad.astype(jnp.float32), axis=0)
    normed_two_grad = against(hidden_grad, fc1_weight)
    shift_two_grad = jnp.sum(normed_two_grad, axis=0)
    scale_two_grad = jnp.sum(normed_two_grad * normed_mid, axis=0)
    middle_grad = upstream + norm_back_two(normed_two_grad * (1.0 + scale_two))[0]
    branch_grad = (valid_rows * gate_one * middle_grad).astype(jnp.bfloat16)
    gate_one_grad = jnp.sum(valid_rows * branch * middle_grad, axis=0)
    proj_w_grad = over_rows(attended, branch_grad)
    proj_b_grad = jnp.sum(branch_grad.astype(jnp.float32), axis=0)
    context_grad = (
        against(branch_grad, proj_weight)
        .astype(jnp.bfloat16)
        .reshape(local_rows, heads_count, head_width)
        * head_keep
    )
    attn_probs = jnp.exp(masked_scores(query_heads, key_heads, allowed, score_scale) - log_total)
    prob_grad = jnp.einsum(
        "qhd,khd->hqk", context_grad, value_heads, preferred_element_type=jnp.float32
    )
    row_total = jnp.sum(attn_probs * prob_grad, axis=-1, keepdims=True)
    score_grad = (attn_probs * (prob_grad - row_total) * score_scale).astype(jnp.bfloat16)
    query_grad = (
        jnp.einsum("hqk,khd->qhd", score_grad, key_heads, preferred_element_type=jnp.float32)
        .reshape(local_rows, model_width)
        .astype(jnp.bfloat16)
    )
    key_part = jnp.einsum(
        "hqk,qhd->khd", score_grad, query_heads, preferred_element_type=jnp.float32
    ).reshape(full_rows, model_width)
    value_part = jnp.einsum(
        "hqk,qhd->khd",
        attn_probs.astype(jnp.bfloat16),
        context_grad,
        preferred_element_type=jnp.float32,
    ).reshape(full_rows, model_width)
    key_sum, value_sum = (
        lax.psum_scatter(
            key_part.astype(jnp.bfloat16), "seq", scatter_dimension=0, tiled=True
        ).astype(jnp.float32),
        lax.psum_scatter(
            value_part.astype(jnp.bfloat16), "seq", scatter_dimension=0, tiled=True
        ).astype(jnp.float32),
    )
    value_low = value_sum.astype(jnp.bfloat16)
    qkv_grad = jnp.concatenate([query_grad, key_sum.astype(jnp.bfloat16), value_low], axis=1)
    qkv_w_grad = over_rows(normed, qkv_grad)
    qv_b_grad = jnp.concatenate(
        [
            jnp.sum(query_grad.astype(jnp.float32), axis=0),
            jnp.sum(value_low.astype(jnp.float32), axis=0),
        ]
    )
    normed_grad = against(qkv_grad, qkv_weight)
    shift_one_grad = jnp.sum(normed_grad, axis=0)
    scale_one_grad = jnp.sum(normed_grad * normed_one, axis=0)
    input_grad = middle_grad + norm_back_one(normed_grad * (1.0 + scale_one))[0]
    mod_part = jnp.concatenate(
        [
            shift_one_grad,
            scale_one_grad,
            gate_one_grad,
            shift_two_grad,
            scale_two_grad,
            gate_two_grad,
        ]
    )
    mod_grad = lax.psum(mod_part, "seq")
    mod_low = mod_grad.astype(jnp.bfloat16)
    cond_grad = silu_back(against(mod_low[None, :], ada_weight)[0])[0]
    ada_w_full = silu_low.astype(jnp.float32)[:, None] * mod_low.astype(jnp.float32)[None, :]
    ada_w_shard, ada_b_shard = (
        lax.psum_scatter(
            ada_w_full.astype(jnp.bfloat16), "bucket", scatter_dimension=0, tiled=True
        ).astype(jnp.float32),
        lax.psum_scatter(
            mod_grad.astype(jnp.bfloat16), "bucket", scatter_dimension=0, tiled=True
        ).astype(jnp.float32),
    )
    all_shards = (
        lax.psum_scatter(
            qkv_w_grad.astype(jnp.bfloat16), "bucket", scatter_dimension=0, tiled=True
        ).astype(jnp.float32),
        lax.psum_scatter(
            qv_b_grad.astype(jnp.bfloat16), "bucket", scatter_dimension=0, tiled=True
        ).astype(jnp.float32),
        lax.psum_scatter(
            proj_w_grad.astype(jnp.bfloat16), "bucket", scatter_dimension=0, tiled=True
        ).astype(jnp.float32),
        lax.psum_scatter(
            proj_b_grad.astype(jnp.bfloat16), "bucket", scatter_dimension=0, tiled=True
        ).astype(jnp.float32),
        lax.psum_scatter(
            fc1_w_grad.astype(jnp.bfloat16), "bucket", scatter_dimension=0, tiled=True
        ).astype(jnp.float32),
        lax.psum_scatter(
            fc1_b_grad.astype(jnp.bfloat16), "bucket", scatter_dimension=0, tiled=True
        ).astype(jnp.float32),
        lax.psum_scatter(
            fc2_w_grad.astype(jnp.bfloat16), "bucket", scatter_dimension=0, tiled=True
        ).astype(jnp.float32),
        lax.psum_scatter(
            fc2_b_grad.astype(jnp.bfloat16), "bucket", scatter_dimension=0, tiled=True
        ).astype(jnp.float32),
    )
    all_shards = (
        lax.psum(all_shards[0].astype(jnp.bfloat16), "seq").astype(jnp.float32),
        lax.psum(all_shards[1].astype(jnp.bfloat16), "seq").astype(jnp.float32),
        lax.psum(all_shards[2].astype(jnp.bfloat16), "seq").astype(jnp.float32),
        lax.psum(all_shards[3].astype(jnp.bfloat16), "seq").astype(jnp.float32),
        lax.psum(all_shards[4].astype(jnp.bfloat16), "seq").astype(jnp.float32),
        lax.psum(all_shards[5].astype(jnp.bfloat16), "seq").astype(jnp.float32),
        lax.psum(all_shards[6].astype(jnp.bfloat16), "seq").astype(jnp.float32),
        lax.psum(all_shards[7].astype(jnp.bfloat16), "seq").astype(jnp.float32),
    )
    (
        qkv_shard,
        qv_shard,
        proj_w_shard,
        proj_b_shard,
        fc1_w_shard,
        fc1_b_shard,
        fc2_w_shard,
        fc2_b_shard,
    ) = all_shards
    return (
        block_out[None],
        input_grad[None],
        cond_grad[None],
        ada_w_shard,
        ada_b_shard,
        qkv_shard,
        qv_shard,
        proj_w_shard,
        proj_b_shard,
        fc1_w_shard,
        fc1_b_shard,
        fc2_w_shard,
        fc2_b_shard,
    )


def solution(mesh):
    return jax.shard_map(
        local,
        mesh=mesh,
        in_specs=(
            P("bucket", "seq", None),
            P("bucket", None),
            P("bucket", None),
            P("bucket", None),
            P("bucket", None),
            P("bucket", "seq"),
            P(),
            P(),
            P(),
            P(),
            P(),
            P(),
            P(),
            P(),
            P(),
            P(),
            P("bucket", "seq", None),
        ),
        out_specs=(
            P("bucket", "seq", None),
            P("bucket", "seq", None),
            P("bucket", None),
            P("bucket", None),
            P("bucket"),
            P("bucket", None),
            P("bucket"),
            P("bucket", None),
            P("bucket"),
            P("bucket", None),
            P("bucket"),
            P("bucket", None),
            P("bucket"),
        ),
        check_vma=False,
    )
```

profile of v0, /device:TPU:0, one launch (start us, length us, event | category | flops | bytes accessed | tf_op | source)
XLA Modules:
  0.0 1146.3 jit_solution(6410899108347407238)
XLA Ops:
  7.2 0.8 convert_element_type.312
  8.1 1.2 convert_reduce_fusion
  9.3 1.3 fusion.52
  10.6 1.3 fusion.117
  11.9 6.4 fusion.71
  19.7 4.7 fusion.104
  24.4 1.7 copy-done.9
  26.0 0.9 slice.42
  27.0 2.6 fusion.59
  29.6 0.6 reduce-scatter.10.cloned.1.call-start
  30.6 0.7 fusion.78
  31.3 0.7 convert_add_fusion.2
  32.2 24.0 %all-gather.5.cloned.1.call-done = bf16[1024,1024]{1,0:T(8,128)(2,1)} async-done(((bf16[256,1024]{1,0:T(8,128)(2,1)}), bf16[1024,1024]{1,0:T(8,128)(2,1)}) %all-gather.5.cloned.1.call-update) | async-done | bytes 2097168 | tf_op jit(solution)/shard_map/all_gather | solution.py:101
  56.2 3.9 copy.43
  60.1 4.5 fusion.4
  64.6 4.4 exponential_reduce_fusion
  69.0 1.8 copy-done.2
  70.8 13.7 %all-gather.3.cloned.1.call-done = bf16[1024,1024]{1,0:T(8,128)(2,1)} async-done(((bf16[256,1024]{1,0:T(8,128)(2,1)}), bf16[1024,1024]{1,0:T(8,128)(2,1)}) %all-gather.3.cloned.1.call-update) | async-done | bytes 2097168 | tf_op jit(solution)/shard_map/all_gather | solution.py:102
  84.5 4.0 copy.41
  88.4 8.7 fusion.46
  97.2 1.8 fusion.113
  99.3 2.5 convolution_add_fusion
  101.9 6.3 fusion.121
  108.3 2.7 multiply_reduce_fusion.1
  111.4 1.0 copy-done.7
  112.9 0.8 copy-done.14
  113.7 1.5 convolution_convert_fusion.5
  115.2 2.0 copy.44
  117.3 11.6 %convolution_convert_fusion.3 = bf16[16,64,1024]{2,1,0:T(8,128)(2,1)} fusion(bf16[256,16,64]{0,2,1:T(8,128)(2,1)} %bitcast.124, bf16[16]{0:T(256)(128)(2,1)S(1)} %get-tuple-element.55, f32[16,256,1024]{2,1,0:T(8,128)} %copy-done.2, f32[16,256]{1,0:T(8,128)S(1)} %log_add_fusion, pred[256,1024]{1,0:T(8,128)(4,1)S(1)} %broadcast_compare_fusion), kind=kOutput, calls=%fused_computation.36 | convolution fusion | flops 554958848 | bytes 19677216 | tf_op jit(solution)/shard_map/hqk,qhd->khd/dot_general | solution.py:157
  128.9 9.8 fusion.63
  138.8 32.0 %fusion.34 = bf16[16,64,1024]{2,1,0:T(8,128)(2,1)} fusion(bf16[256,16,64]{0,2,1:T(8,128)(2,1)} %bitcast.123, f32[16,256,1024]{2,1,0:T(8,128)} %fusion.63, f32[16,256,1024]{2,1,0:T(8,128)} %copy-done.2, f32[16,256]{1,0:T(8,128)S(1)} %log_add_fusion, pred[256,1024]{1,0:T(8,128)(4,1)S(1)} %broadcast_compare_fusion), kind=kOutput, calls=%fused_computation.37 | convolution fusion | flops 584061952 | bytes 36454400 | tf_op jit(solution)/shard_map/hqk,qhd->khd/dot_general | solution.py:154
  170.8 3.4 convolution_convert_fusion.4
  174.3 6.0 convolution_convert_fusion.1
  180.3 1.1 copy-done.17
  181.4 9.1 convolution_convert_fusion
  190.6 30.9 %fusion.118 = (bf16[16,64]{1,0:T(8,128)(2,1)S(1)}, bf16[16,64,256]{2,1,0:T(8,128)(2,1)S(1)}) fusion(bf16[1024,16,64]{0,2,1:T(8,128)(2,1)} %bitcast.119, f32[16,256,1024]{2,1,0:T(8,128)} %fusion.63, f32[16,256,1024]{2,1,0:T(8,128)} %copy-done.2, f32[16,256]{1,0:T(8,128)S(1)} %log_add_fusion, pred[256,1024]{1,0:T(8,128)(4,1)S(1)} %broadcast_compare_fusion), kind=kOutput, calls=%fused_computation.164 | convolution fusion | flops 583536640 | bytes 36456448 | tf_op jit(solution)/shard_map/hqk,khd->qhd/dot_general | solution.py:150
  221.6 6.1 convolution_convert_fusion.2
  227.8 0.6 copy-done.19
  228.4 5.4 fusion.53
  233.9 0.6 fusion.51
  234.5 8.2 fusion.58
  242.8 14.0 %psum.63 = bf16[6144]{0:T(1024)(128)(2,1)S(1)} all-reduce(f32[6144]{0:T(1024)S(1)} %constant_dynamic-update-slice_fusion), channel_id=1, replica_groups=mesh['bucket'=32,'seq'=4] {'seq'}, use_global_device_ids=true, to_apply=%region_19.20 | all-reduce | flops 6144 | bytes 36864 | tf_op jit(solution)/shard_map/psum | solution.py:194
  256.8 8.0 fusion.122
  264.7 0.6 fusion.76
  265.4 108.6 %reduce-scatter.16.cloned.1.call-done = bf16[32,1024]{1,0:T(8,128)(2,1)} async-done(((bf16[1024,1024]{1,0:T(8,128)(2,1)}), bf16[32,1024]{1,0:T(8,128)(2,1)}) %reduce-scatter.16.cloned.1.call-update) | async-done | bytes 65552 | tf_op jit(solution)/shard_map/reduce_scatter | solution.py:213
  373.9 177.3 %reduce-scatter.18.cloned.1.call-done = bf16[32,4096]{1,0:T(8,128)(2,1)} async-done(((bf16[1024,4096]{1,0:T(8,128)(2,1)}), bf16[32,4096]{1,0:T(8,128)(2,1)}) %reduce-scatter.18.cloned.1.call-update) | async-done | bytes 262160 | tf_op jit(solution)/shard_map/reduce_scatter | solution.py:219
  551.2 177.5 %reduce-scatter.20.cloned.1.call-done = bf16[128,1024]{1,0:T(8,128)(2,1)} async-done(((bf16[4096,1024]{1,0:T(8,128)(2,1)}), bf16[128,1024]{1,0:T(8,128)(2,1)}) %reduce-scatter.20.cloned.1.call-update) | async-done | bytes 262160 | tf_op jit(solution)/shard_map/reduce_scatter | solution.py:225
  728.7 172.9 %reduce-scatter.14.cloned.1.call-done = bf16[32,3072]{1,0:T(8,128)(2,1)} async-done(((bf16[1024,3072]{1,0:T(8,128)(2,1)}), bf16[32,3072]{1,0:T(8,128)(2,1)}) %reduce-scatter.14.cloned.1.call-update) | async-done | bytes 196624 | tf_op jit(solution)/shard_map/reduce_scatter | solution.py:207
  901.7 7.5 multiply_convert_fusion
  909.3 0.6 copy-done.28
  909.9 0.6 dynamic-slice
  913.4 153.1 %all-reduce.5 = (bf16[6144]{0:T(1024)(128)(2,1)S(1)}, bf16[2048]{0:T(1024)(128)(2,1)S(1)}, bf16[1024]{0:T(1024)(128)(2,1)S(1)}, bf16[4096]{0:T(1024)(128)(2,1)S(1)}, bf16[1024]{0:T(1024)(128)(2,1)S(1)}) all-reduce(bf16[6144]{0:T(1024)(128)(2,1)S(1)} %psum.63, ...), channel_id=5, replica_groups=mesh['bucket'=32,'seq'=4] {'bucket'}, use_global_device_ids=true, to_apply=%region_21.22.clone | all-reduce | flops 14336 | bytes 57344
  1066.8 7.5 all-reduce.6
  1074.4 0.5 convert_element_type.349
  1074.9 0.5 convert_element_type.352
  1075.4 0.5 convert_element_type.355
  1075.9 0.5 convert_element_type.358
  1076.4 0.6 dynamic-slice_convert_fusion
  1077.1 1.5 convert_element_type.351
  1078.6 1.7 convert_element_type.346
  1080.3 1.8 convert_element_type.354
  1082.0 1.8 convert_element_type.357
  1083.8 53.5 %reduce-scatter.12.cloned.1.call-done = bf16[32,6144]{1,0:T(8,128)(2,1)} async-done(((bf16[1024,6144]{1,0:T(8,128)(2,1)}), bf16[32,6144]{1,0:T(8,128)(2,1)}) %reduce-scatter.12.cloned.1.call-update) | async-done | bytes 393232 | tf_op jit(solution)/shard_map/reduce_scatter | solution.py:199
  1137.4 1.9 convert_element_type.343
  (128 shorter events, 3.1 us)
Async XLA Ops:
  7.2 90.0 %copy-start = (bf16[1024,1024]{1,0:T(8,128)(2,1)S(1)}, bf16[1024,1024]{1,0:T(8,128)(2,1)}, u32[]{:S(2)}) copy-start(bf16[1024,1024]{1,0:T(8,128)(2,1)} %param.27) | copy-start | bytes 6291460
  7.2 49.0 %all-gather.5.cloned.1.call-start = ((), (), s32[]{:S(2)}) async-start(), calls=%async_computation.8 | async-start | bytes 2621440 | tf_op jit(solution)/shard_map/all_gather | solution.py:101
  11.9 6.4 copy-start.21
  11.9 7.7 copy-start.3
  19.6 7.3 copy-start.20
  24.4 1.7 copy-start.9
  26.0 4.2 copy-start.25
  26.0 4.2 copy-start.23
  26.0 4.3 copy-start.22
  26.0 5.9 copy-start.26
  26.9 57.6 %all-gather.3.cloned.1.call-start = ((), (), s32[]{:S(2)}) async-start(), calls=%async_computation.7 | async-start | bytes 2621440 | tf_op jit(solution)/shard_map/all_gather | solution.py:102
  29.6 192.0 %reduce-scatter.10.cloned.1.call-start = ((), (), s32[]{:S(2)}) async-start(), calls=%async_computation.10 | async-start | bytes 2621440 | tf_op jit(solution)/shard_map/reduce_scatter | solution.py:167
  30.5 34.0 %copy-start.12 = (bf16[256,1024]{0,1:T(8,128)(2,1)}, bf16[256,1024]{0,1:T(8,128)(2,1)S(1)}, u32[]{:S(2)}) copy-start(bf16[256,1024]{0,1:T(8,128)(2,1)S(1)} %copy.42) | copy-start | bytes 1572868
  64.6 6.2 copy-start.2
  88.4 10.8 slice-start
  88.4 8.8 copy-start.4
  88.4 10.8 slice-start.1
  97.2 4.7 copy-start.13
  97.2 4.7 slice-start.2
  99.3 2.6 copy-start.16
  99.3 2.6 slice-start.3
  101.9 6.4 copy-start.29
  108.3 2.7 copy-start.10
  111.4 1.0 copy-start.7
  112.9 0.8 copy-start.14
  117.3 11.7 %copy-start.6 = (bf16[1024,1024]{0,1:T(8,128)(2,1)S(1)}, bf16[1024,1024]{0,1:T(8,128)(2,1)}, u32[]{:S(2)}) copy-start(bf16[1024,1024]{0,1:T(8,128)(2,1)} %copy.41) | copy-start | bytes 6291460
  128.9 92.8 %reduce-scatter.8.cloned.1.call-start = ((), (), s32[]{:S(2)}) async-start(), calls=%async_computation.9 | async-start | bytes 2621440 | tf_op jit(solution)/shard_map/reduce_scatter | solution.py:164
  170.7 3.6 copy-start.11
  170.7 203.2 %reduce-scatter.16.cloned.1.call-start = ((), (), s32[]{:S(2)}) async-start(), calls=%async_computation.13 | async-start | bytes 2162688 | tf_op jit(solution)/shard_map/reduce_scatter | solution.py:213
  174.2 377.0 %reduce-scatter.18.cloned.1.call-start = ((), (), s32[]{:S(2)}) async-start(), calls=%async_computation.14 | async-start | bytes 8650752 | tf_op jit(solution)/shard_map/reduce_scatter | solution.py:219
  180.3 1.1 copy-start.17
  180.3 548.5 %reduce-scatter.20.cloned.1.call-start = ((), (), s32[]{:S(2)}) async-start(), calls=%async_computation.15 | async-start | bytes 8650752 | tf_op jit(solution)/shard_map/reduce_scatter | solution.py:225
  190.6 31.1 %copy-start.5 = (bf16[1,256,1024]{2,1,0:T(8,128)(2,1)S(1)}, bf16[1,256,1024]{2,1,0:T(8,128)(2,1)}, u32[]{:S(2)}) copy-start(bf16[1,256,1024]{2,1,0:T(8,128)(2,1)} %param.17) | copy-start | bytes 1572868
  190.6 711.1 %reduce-scatter.14.cloned.1.call-start = ((), (), s32[]{:S(2)}) async-start(), calls=%async_computation.12 | async-start | bytes 6488064 | tf_op jit(solution)/shard_map/reduce_scatter | solution.py:207
  221.6 6.1 copy-start.27
  227.7 0.7 copy-start.19
  227.7 0.7 copy-start.24
  227.7 849.3 %all-reduce.10.cloned.1.call-start = ((), (), s32[]{:S(2)}) async-start(), calls=%async_computation.16 | async-start | bytes 1572864 | tf_op jit(solution)/shard_map/psum | solution.py:233
  228.4 6.1 copy-start.8
  228.4 6.1 copy-start.15
  228.4 6.1 copy-start.30
  901.7 235.7 %reduce-scatter.12.cloned.1.call-start = ((), (), s32[]{:S(2)}) async-start(), calls=%async_computation.11 | async-start | bytes 12976128 | tf_op jit(solution)/shard_map/reduce_scatter | solution.py:199
  909.3 0.7 copy-start.28
  909.3 3.9 copy-start.18
  909.3 230.0 %copy-start.1 = (bf16[1024,1024]{1,0:T(8,128)(2,1)S(1)}, bf16[1024,1024]{1,0:T(8,128)(2,1)}, u32[]{:S(2)}) copy-start(bf16[1024,1024]{1,0:T(8,128)(2,1)} %param.27) | copy-start | bytes 6291460
Sparse Core Ops, SparseCore 0:
  27.0 29.0 all-gather.4
  58.4 26.0 all-gather.2
  129.0 37.7 reduce-scatter.9
  170.9 37.7 reduce-scatter.7
  210.9 163.0 reduce-scatter.15
  376.3 174.8 reduce-scatter.17
  553.7 174.9 reduce-scatter.19
  731.3 170.3 reduce-scatter.13
  904.7 39.8 all-reduce.9
  946.9 190.3 reduce-scatter.11
where the time goes:
time: 1150 us
  waiting for transfers between devices  728 us (63%)
  blocking collectives  175 us (15%)
  matrix products  170 us (15%)
  other arithmetic  33.5 us (3%)
  local copies, waits for them, and re-layouts  21.1 us (2%)
  between operations  18.9 us (2%)
    reduce_scatter x1, waiting for transfers between devices, local(): lax.psum_scatter(fc2_w_grad.astype(jnp.bfloat16), 'bucket', scatter_dimen...  178 us
    reduce_scatter x1, waiting for transfers between devices, local(): lax.psum_scatter(fc1_w_grad.astype(jnp.bfloat16), 'bucket', scatter_dimen...  177 us
    reduce_scatter x1, waiting for transfers between devices, local(): lax.psum_scatter(qkv_w_grad.astype(jnp.bfloat16), 'bucket', scatter_dimen...  173 us
    unnamed x1, blocking collectives  153 us
    reduce_scatter x1, waiting for transfers between devices, local(): lax.psum_scatter(proj_w_grad.astype(jnp.bfloat16), 'bucket', scatter_dime...  109 us
    reduce_scatter x1, waiting for transfers between devices, local(): lax.psum_scatter(ada_w_full.astype(jnp.bfloat16), 'bucket', scatter_dimen...  53.5 us
    dot_general x1, matrix products, local(): jnp.einsum('hqk,qhd->khd', score_grad, query_heads, preferred_element_typ...  32 us
    dot_general x1, matrix products, local(): jnp.einsum('hqk,khd->qhd', score_grad, key_heads, preferred_element_type=...  30.9 us
  transfers between devices with their start and end apart: 10, of which 7 were waited for; matrix products, arithmetic and copies ran while one was open for 14% of the time, Pallas kernels for 0%

commit v1 on v0

--- a/solution.py
+++ b/solution.py
@@ -1,7 +1,246 @@
+import functools
+
 import jax
 import jax.numpy as jnp
 from jax import lax
+from jax.experimental import pallas as pl
+from jax.experimental.pallas import tpu as pltpu
 from jax.sharding import PartitionSpec as P
+
+
+MESH_IDS = pl.DeviceIdType.MESH
+AXES = {"x": 0, "y": 1, "z": 2}
+ROUTES = ("zyx", "yxz", "xzy")
+
+
+def place():
+    bucket = lax.axis_index("bucket")
+    seq = lax.axis_index("seq")
+    return (
+        (seq // 2) * 2 + (bucket // 4) % 2,
+        bucket % 4,
+        bucket // 8,
+        seq % 2,
+    )
+
+
+def device(x, y, z, core):
+    return (z * 8 + (x % 2) * 4 + y, (x // 2) * 2 + core)
+
+
+def shifted(spot, axis, step):
+    x, y, z, core = spot
+    if axis == "x":
+        x = (x + step) % 4
+    elif axis == "y":
+        y = (y + step) % 4
+    elif axis == "z":
+        z = (z + step) % 4
+    else:
+        core = 1 - core
+    return device(x, y, z, core)
+
+
+def greet(spot, moves):
+    barrier = pltpu.get_barrier_semaphore()
+    for axis, step in moves:
+        pl.semaphore_signal(
+            barrier, inc=1, device_id=shifted(spot, axis, step), device_id_type=MESH_IDS
+        )
+    pl.semaphore_wait(barrier, len(moves))
+
+
+TORUS = [(axis, step) for axis in "xyz" for step in (1, -1)]
+
+
+def cut(route, phase, target, spot):
+    index = {"z": slice(None), "x": (slice(None), slice(None)), "y": slice(None)}
+    axis = route[phase]
+    index[axis] = (target % 2, target // 2) if axis == "x" else target
+    done = route[:phase]
+    parts = []
+    if "z" not in done:
+        parts.append(index["z"])
+    if "x" not in done:
+        parts.append(index["x"][0])
+    if "y" not in done:
+        parts.append(index["y"])
+    if "x" not in done:
+        parts.append(index["x"][1])
+    return tuple(parts)
+
+
+def left_over(route, phase):
+    done = route[:phase]
+    dims = []
+    if "z" not in done:
+        dims.append(4)
+    if "x" not in done:
+        dims.append(2)
+    if "y" not in done:
+        dims.append(4)
+    if "x" not in done:
+        dims.append(2)
+    return tuple(dims)
+
+
+class Piece:
+    def __init__(self, source, columns, route, landing, sums, send_sem, recv_sem, spot):
+        self.source, self.columns, self.route = source, columns, route
+        self.landing, self.sums = landing, sums
+        self.send_sem, self.recv_sem, self.spot = send_sem, recv_sem, spot
+        self.copies = {}
+
+    def block(self, phase, target, half):
+        width = self.columns // 2
+        index = cut(self.route, phase, target, self.spot)
+        lanes = pl.ds(half * width, width)
+        if phase == 0:
+            return self.source(index, half * width, width)
+        return self.sums[phase - 1].at[index + (slice(None), lanes)]
+
+    def here(self, phase):
+        return self.spot[AXES[self.route[phase]]]
+
+    def send(self, phase, slot, ref, step):
+        copy = pltpu.make_async_remote_copy(
+            src_ref=ref,
+            dst_ref=self.landing[phase].at[slot],
+            send_sem=self.send_sem.at[phase, slot],
+            recv_sem=self.recv_sem.at[phase, slot],
+            device_id=shifted(self.spot, self.route[phase], step),
+            device_id_type=MESH_IDS,
+        )
+        copy.start()
+        self.copies[phase, slot] = copy
+
+    def first(self, phase):
+        a = self.here(phase)
+        self.send(phase, 0, self.block(phase, (a + 2) % 4, 0), 1)
+        self.send(phase, 1, self.block(phase, (a + 2) % 4, 1), -1)
+        self.send(phase, 2, self.block(phase, (a + 1) % 4, 1), 1)
+        self.send(phase, 3, self.block(phase, (a + 3) % 4, 0), -1)
+
+    def second(self, phase):
+        a = self.here(phase)
+        landing = self.landing[phase]
+        for slot, step, half in ((0, 1, 0), (1, -1, 1)):
+            self.copies[phase, slot].wait_recv()
+            add_into(landing.at[slot], [self.block(phase, (a + step) % 4, half)])
+            self.send(phase, slot + 4, landing.at[slot], step)
+
+    def third(self, phase):
+        a = self.here(phase)
+        landing = self.landing[phase]
+        width = self.columns // 2
+        for slot in (2, 3, 4, 5):
+            self.copies[phase, slot].wait_recv()
+        for half, slots in ((0, (3, 4)), (1, (2, 5))):
+            target = self.sums[phase].at[..., pl.ds(half * width, width)]
+            add_into(
+                target,
+                [landing.at[slots[0]], landing.at[slots[1]]],
+                self.block(phase, a, half),
+            )
+
+    def finish(self):
+        for copy in self.copies.values():
+            copy.wait_send()
+
+
+def add_into(target, others, start=None):
+    total = (target if start is None else start)[...].astype(jnp.float32)
+    for other in others:
+        total = total + other[...].astype(jnp.float32)
+    target[...] = total.astype(jnp.bfloat16)
+
+
+def reduce_kernel(views, *refs):
+    count = len(views)
+    inputs = max(v[0] for v in views) + 1
+    sources, outs = refs[:inputs], refs[inputs : inputs + count]
+    scratch = list(refs[inputs + count :])
+    send_sem, recv_sem, end_send, end_recv = scratch[-4:]
+    spot = place()
+    greet(spot, TORUS + [("core", 0), ("x", 2)])
+    pieces = []
+    for k, (which, kind, offset, columns) in enumerate(views):
+        landing, sums = scratch[8 * k : 8 * k + 3], scratch[8 * k + 3 : 8 * k + 6]
+
+        def source(index, start, width, ref=sources[which], kind=kind, offset=offset):
+            if kind == "rows":
+                return ref.at[index + (offset, slice(None), pl.ds(start, width))]
+            return ref.at[index + (slice(None), pl.ds(offset + start, width))]
+
+        pieces.append(
+            Piece(
+                source, columns, ROUTES[k % 3], landing, sums, send_sem.at[k], recv_sem.at[k], spot
+            )
+        )
+    for piece in pieces:
+        piece.first(0)
+    for phase in range(3):
+        for piece in pieces:
+            piece.second(phase)
+        for piece in pieces:
+            piece.third(phase)
+            if phase < 2:
+                piece.first(phase + 1)
+
+    def to(k, stage, src, dst, axis, step):
+        copy = pltpu.make_async_remote_copy(
+            src_ref=src,
+            dst_ref=dst,
+            send_sem=end_send.at[k, stage],
+            recv_sem=end_recv.at[k, stage],
+            device_id=shifted(spot, axis, step),
+            device_id_type=MESH_IDS,
+        )
+        copy.start()
+        return copy
+
+    near, far = [], []
+    for k, piece in enumerate(pieces):
+        near.append(to(k, 0, piece.sums[2], scratch[8 * k + 6], "core", 0))
+    high = spot[0] // 2
+    for k, piece in enumerate(pieces):
+        near[k].wait()
+        both, there = scratch[8 * k + 6], scratch[8 * k + 7]
+        add_into(both, [piece.sums[2]])
+        far.append(to(k, 1, both, there, "x", 2))
+        outs[k][high] = both[...].astype(jnp.float32)
+    for k, piece in enumerate(pieces):
+        far[k].wait()
+        outs[k][1 - high] = scratch[8 * k + 7][...].astype(jnp.float32)
+    for piece in pieces:
+        piece.finish()
+
+
+def reduce_weights(arrays, views, collective_id, name):
+    scratch = []
+    for k, (_, _, _, columns) in enumerate(views):
+        route = ROUTES[k % 3]
+        dims = [left_over(route, phase) + (16,) for phase in range(4)]
+        for phase in range(3):
+            scratch.append(pltpu.VMEM((6,) + dims[phase + 1] + (columns // 2,), jnp.bfloat16))
+        for phase in range(3):
+            scratch.append(pltpu.VMEM(dims[phase + 1] + (columns,), jnp.bfloat16))
+        scratch.append(pltpu.VMEM((16, columns), jnp.bfloat16))
+        scratch.append(pltpu.VMEM((16, columns), jnp.bfloat16))
+    count = len(views)
+    scratch += [pltpu.SemaphoreType.DMA((count, 3, 6))] * 2
+    scratch += [pltpu.SemaphoreType.DMA((count, 2))] * 2
+    return pl.pallas_call(
+        functools.partial(reduce_kernel, views),
+        out_shape=[jax.ShapeDtypeStruct((2, 16, v[3]), jnp.float32) for v in views],
+        in_specs=[pl.BlockSpec(memory_space=pltpu.VMEM)] * len(arrays),
+        out_specs=[pl.BlockSpec(memory_space=pltpu.VMEM)] * count,
+        scratch_shapes=scratch,
+        compiler_params=pltpu.CompilerParams(
+            collective_id=collective_id, has_side_effects=True, vmem_limit_bytes=60 << 20
+        ),
+        name=name,
+    )(*arrays)
 
 
 def normalize(values):
@@ -194,61 +433,47 @@
     mod_grad = lax.psum(mod_part, "seq")
     mod_low = mod_grad.astype(jnp.bfloat16)
     cond_grad = silu_back(against(mod_low[None, :], ada_weight)[0])[0]
-    ada_w_full = silu_low.astype(jnp.float32)[:, None] * mod_low.astype(jnp.float32)[None, :]
-    ada_w_shard, ada_b_shard = (
-        lax.psum_scatter(
-            ada_w_full.astype(jnp.bfloat16), "bucket", scatter_dimension=0, tiled=True
-        ).astype(jnp.float32),
-        lax.psum_scatter(
-            mod_grad.astype(jnp.bfloat16), "bucket", scatter_dimension=0, tiled=True
-        ).astype(jnp.float32),
-    )
-    all_shards = (
-        lax.psum_scatter(
-            qkv_w_grad.astype(jnp.bfloat16), "bucket", scatter_dimension=0, tiled=True
-        ).astype(jnp.float32),
-        lax.psum_scatter(
-            qv_b_grad.astype(jnp.bfloat16), "bucket", scatter_dimension=0, tiled=True
-        ).astype(jnp.float32),
-        lax.psum_scatter(
-            proj_w_grad.astype(jnp.bfloat16), "bucket", scatter_dimension=0, tiled=True
-        ).astype(jnp.float32),
-        lax.psum_scatter(
-            proj_b_grad.astype(jnp.bfloat16), "bucket", scatter_dimension=0, tiled=True
-        ).astype(jnp.float32),
-        lax.psum_scatter(
-            fc1_w_grad.astype(jnp.bfloat16), "bucket", scatter_dimension=0, tiled=True
-        ).astype(jnp.float32),
-        lax.psum_scatter(
-            fc1_b_grad.astype(jnp.bfloat16), "bucket", scatter_dimension=0, tiled=True
-        ).astype(jnp.float32),
-        lax.psum_scatter(
-            fc2_w_grad.astype(jnp.bfloat16), "bucket", scatter_dimension=0, tiled=True
-        ).astype(jnp.float32),
-        lax.psum_scatter(
-            fc2_b_grad.astype(jnp.bfloat16), "bucket", scatter_dimension=0, tiled=True
-        ).astype(jnp.float32),
-    )
-    all_shards = (
-        lax.psum(all_shards[0].astype(jnp.bfloat16), "seq").astype(jnp.float32),
-        lax.psum(all_shards[1].astype(jnp.bfloat16), "seq").astype(jnp.float32),
-        lax.psum(all_shards[2].astype(jnp.bfloat16), "seq").astype(jnp.float32),
-        lax.psum(all_shards[3].astype(jnp.bfloat16), "seq").astype(jnp.float32),
-        lax.psum(all_shards[4].astype(jnp.bfloat16), "seq").astype(jnp.float32),
-        lax.psum(all_shards[5].astype(jnp.bfloat16), "seq").astype(jnp.float32),
-        lax.psum(all_shards[6].astype(jnp.bfloat16), "seq").astype(jnp.float32),
-        lax.psum(all_shards[7].astype(jnp.bfloat16), "seq").astype(jnp.float32),
-    )
-    (
-        qkv_shard,
-        qv_shard,
-        proj_w_shard,
-        proj_b_shard,
-        fc1_w_shard,
-        fc1_b_shard,
-        fc2_w_shard,
-        fc2_b_shard,
-    ) = all_shards
+    silu_all = lax.all_gather(silu_low, "bucket", axis=0)
+    mod_all = lax.all_gather(mod_low, "bucket", axis=0)
+    bucket = lax.axis_index("bucket")
+    width = model_width // 32
+    silu_mine = lax.dynamic_slice_in_dim(silu_all, bucket * width, width, axis=1)
+    ada_w_shard = over_rows(silu_mine, mod_all)
+    vectors = jnp.concatenate([qv_b_grad, proj_b_grad, fc1_b_grad, fc2_b_grad])
+    vectors = lax.psum(vectors, ("bucket", "seq"))
+    sizes = (2 * model_width, model_width, fc1_weight.shape[1], model_width)
+    shards, start = [], 0
+    for size in sizes:
+        shards.append(lax.dynamic_slice_in_dim(vectors, start + bucket * (size // 32), size // 32))
+        start += size
+    qv_shard, proj_b_shard, fc1_b_shard, fc2_b_shard = shards
+    ada_b_shard = lax.dynamic_slice_in_dim(
+        jnp.sum(mod_all.astype(jnp.float32), axis=0), bucket * 6 * width, 6 * width
+    )
+    grid = (4, 2, 4, 2)
+    fc2_pieces = reduce_weights(
+        [
+            fc2_w_grad.astype(jnp.bfloat16).reshape(grid + (4, 16, model_width)),
+            proj_w_grad.astype(jnp.bfloat16).reshape(grid + (16, model_width)),
+        ],
+        [(0, "rows", q, model_width) for q in range(4)] + [(1, "columns", 0, model_width)],
+        0,
+        "reduce_fc2_proj",
+    )
+    fc1_pieces = reduce_weights(
+        [
+            fc1_w_grad.astype(jnp.bfloat16).reshape(grid + (16, 4 * model_width)),
+            qkv_w_grad.astype(jnp.bfloat16).reshape(grid + (16, 3 * model_width)),
+        ],
+        [(0, "columns", q * model_width, model_width) for q in range(4)]
+        + [(1, "columns", q * model_width, model_width) for q in range(3)],
+        1,
+        "reduce_fc1_qkv",
+    )
+    fc2_w_shard = jnp.stack(fc2_pieces[:4], axis=1).reshape(128, model_width)
+    proj_w_shard = fc2_pieces[4].reshape(32, model_width)
+    fc1_w_shard = jnp.concatenate(fc1_pieces[:4], axis=2).reshape(32, 4 * model_width)
+    qkv_shard = jnp.concatenate(fc1_pieces[4:], axis=2).reshape(32, 3 * model_width)
     return (
         block_out[None],
         input_grad[None],

time: 1150 us -> 667 us (0.58)
  waiting for transfers between devices: 728 us -> 35.6 us
  Pallas kernels: 0 us -> 154 us
  blocking collectives: 175 us -> 240 us
  other arithmetic: 33.5 us -> 18 us
    reduce_scatter x5 -> x0, waiting for transfers between devices: 690 us -> none  [the longest x1 178 us: local(): lax.psum_scatter(fc2_w_grad.astype(jnp.bfloat16), 'bucket', scatter_dimen...]
    all_gather x0 -> x2, blocking collectives: none -> 163 us  [the longest x1 81.9 us: local(): silu_all = lax.all_gather(silu_low, 'bucket', axis=0)]
    pallas_call x0 -> x2, Pallas kernels: none -> 154 us  [reduce_weights(): pl.pallas_call(functools.partial(reduce_kernel, views), out_shape=[jax.Sh...]
    unnamed x1 -> x0, blocking collectives: 153 us -> none
    psum x1, blocking collectives: 7.54 us -> 62.9 us  [local(): vectors = lax.psum(vectors, ('bucket', 'seq'))]
    convert_element_type x13 -> x0, other arithmetic: 19.6 us -> none  [the longest x1 7.54 us: local(): ada_w_full.astype(jnp.bfloat16)]
    dot_general x4 -> x5, matrix products: 24.6 us -> 24.4 us  [over_rows(): lax.dot_general(first_op, second_op, (((0,), (0,)), ((), ())), preferred_...]
  transfers between devices with their start and end apart: 10 -> 4, of which waited for: 7 -> 2; matrix products, arithmetic and copies ran while one was open for 14% -> 13% of each run, Pallas kernels for 0% -> 10%
where the time goes in v1:
time: 667 us; the launch traced here: 662 us
  blocking collectives  240 us (36%)
  matrix products  178 us (27%)
  Pallas kernels  154 us (23%)
  waiting for transfers between devices  35.6 us (5%)
  local copies, waits for them, and re-layouts  19.8 us (3%)
  other arithmetic  18 us (3%)
  between operations  16.1 us (2%)
    pallas_call x2, Pallas kernels, reduce_weights(): pl.pallas_call(functools.partial(reduce_kernel, views), out_shape=[jax.Sh...  154 us
    all_gather x1, blocking collectives, local(): silu_all = lax.all_gather(silu_low, 'bucket', axis=0)  81.9 us
    all_gather x1, blocking collectives, local(): mod_all = lax.all_gather(mod_low, 'bucket', axis=0)  81.4 us
    psum x1, blocking collectives, local(): vectors = lax.psum(vectors, ('bucket', 'seq'))  62.9 us
    dot_general x1, matrix products, local(): jnp.einsum('hqk,qhd->khd', score_grad, query_heads, preferred_element_typ...  39.4 us
    dot_general x1, matrix products, local(): jnp.einsum('hqk,khd->qhd', score_grad, key_heads, preferred_element_type=...  38.2 us
    dot_general x5, matrix products, over_rows(): lax.dot_general(first_op, second_op, (((0,), (0,)), ((), ())), preferred_...  24.4 us
    dot_general x5, matrix products, against(): lax.dot_general(first_op, second_op, (((1,), (1,)), ((), ())), preferred_...  24 us
  transfers between devices with their start and end apart: 4, of which 2 were waited for; matrix products, arithmetic and copies ran while one was open for 13% of the time, Pallas kernels for 10%

profile of v1, /device:TPU:0, one launch (start us, length us, event | category | flops | bytes accessed | tf_op | source)
XLA Modules:
  0.0 662.4 jit_solution(3759540983903174073)
XLA Ops:
  7.3 6.5 fusion.72
  13.8 0.1 convert_reduce_fusion.1
  13.9 0.3 fusion.52
  14.3 1.9 fusion.99
  16.2 1.7 copy-done.9
  17.9 0.9 slice.42
  18.9 2.6 fusion.59
  21.5 0.2 reduce-scatter.3.cloned.1.call-start
  21.8 0.6 fusion.111
  22.4 0.2 copy.49
  24.1 0.7 fusion.75
  24.7 0.7 convert_add_fusion.2
  25.4 0.5 convert_bitcast_fusion.3
  25.9 0.2 broadcast_compare_fusion
  26.1 21.9 %all-gather.7.cloned.1.call-done = bf16[1024,1024]{1,0:T(8,128)(2,1)} async-done(((bf16[256,1024]{1,0:T(8,128)(2,1)}), bf16[1024,1024]{1,0:T(8,128)(2,1)}) %all-gather.7.cloned.1.call-update) | async-done | bytes 2097168 | tf_op jit(solution)/shard_map/all_gather | solution.py:340
  48.0 4.0 copy.50
  52.0 4.5 fusion.4
  56.5 4.4 exponential_reduce_fusion
  60.9 1.8 copy-done.2
  62.7 13.6 %all-gather.5.cloned.1.call-done = bf16[1024,1024]{1,0:T(8,128)(2,1)} async-done(((bf16[256,1024]{1,0:T(8,128)(2,1)}), bf16[1024,1024]{1,0:T(8,128)(2,1)}) %all-gather.5.cloned.1.call-update) | async-done | bytes 2097168 | tf_op jit(solution)/shard_map/all_gather | solution.py:341
  76.4 3.9 copy.48
  80.3 8.7 %fusion.46 = bf16[16,64,256]{2,1,0:T(8,128)(2,1)S(1)} fusion(bf16[1024,16,64]{0,2,1:T(8,128)(2,1)} %bitcast.140, f32[16]{0:T(128)S(1)} %get-tuple-element.68, f32[16,256,1024]{2,1,0:T(8,128)} %copy-done.2, f32[16,256]{1,0:T(8,128)S(1)} %log_add_fusion, pred[256,1024]{1,0:T(8,128)(4,1)S(1)} %broadcast_compare_fusion), kind=kOutput, calls=%fused_computation.61 | convolution fusion | flops 554172416 | bytes 19677248 | tf_op jit(solution)/shard_map/hqk,khd->qhd/dot_general | solution.py:350
  89.1 0.9 fusion.106
  90.0 0.3 multiply_reduce_fusion.4
  90.3 2.5 convolution_add_fusion
  92.9 0.2 slice-done.3
  93.1 6.3 convert_reduce_fusion
  99.4 2.9 multiply_reduce_fusion.1
  102.4 0.4 fusion.105
  102.8 7.0 %convert_reduce_fusion.2 = (f32[1024]{0:T(1024)S(1)}, f32[1024]{0:T(1024)S(1)}, f32[1024]{0:T(1024)S(1)}, f32[1024]{0:T(1024)S(1)}, bf16[256,1024]{1,0:T(8,128)(2,1)S(1)}, /*index=5*/f32[1,256,1024]{2,1,0:T(8,128)}) fusion(bf16[1,256,1024]{2,1,0:T(8,128)(2,1)S(1)} %copy-done.15, f32[1024]{0:T(1024)S(1)} %get-tuple-element.59, f32[256]{0:T(256)S(1)} %fusion.77, ...), kind=kOutput, calls=%fused_computation.79 | convolution fusion | flops 2163732480 | bytes 17873920 | tf_op jit(solution)/shard_map/dot_general | solution.py:260
  109.8 0.8 copy-done.20
  110.6 1.5 convolution_convert_fusion.5
  112.2 1.2 copy.51
  113.5 9.8 %fusion.63 = f32[16,256,1024]{2,1,0:T(8,128)} fusion(bf16[1024,16,64]{0,2,1:T(8,128)(2,1)} %bitcast.141, bf16[256,16,64]{0,2,1:T(8,128)(2,1)S(1)} %bitcast.145, bf16[16]{0:T(256)(128)(2,1)S(1)} %copy-done.31), kind=kOutput, calls=%fused_computation.95 | convolution fusion | flops 537133056 | bytes 19398688 | tf_op jit(solution)/shard_map/qhd,khd->hqk/dot_general | solution.py:383
  123.3 39.4 %fusion.34 = bf16[16,64,1024]{2,1,0:T(8,128)(2,1)} fusion(bf16[256,16,64]{0,2,1:T(8,128)(2,1)S(1)} %bitcast.144, f32[16,256,1024]{2,1,0:T(8,128)} %fusion.63, f32[16,256,1024]{2,1,0:T(8,128)} %copy-done.2, f32[16,256]{1,0:T(8,128)S(1)} %log_add_fusion, pred[256,1024]{1,0:T(8,128)(4,1)S(1)} %broadcast_compare_fusion), kind=kOutput, calls=%fused_computation.37 | convolution fusion | flops 584061952 | bytes 36454400 | tf_op jit(solution)/shard_map/hqk,qhd->khd/dot_general | solution.py:393
  162.8 9.9 %convolution_convert_fusion.3 = bf16[16,64,1024]{2,1,0:T(8,128)(2,1)} fusion(bf16[256,16,64]{0,2,1:T(8,128)(2,1)S(1)} %bitcast.146, bf16[16]{0:T(256)(128)(2,1)S(1)} %copy-done.31, f32[16,256,1024]{2,1,0:T(8,128)} %copy-done.2, f32[16,256]{1,0:T(8,128)S(1)} %log_add_fusion, pred[256,1024]{1,0:T(8,128)(4,1)S(1)} %broadcast_compare_fusion), kind=kOutput, calls=%fused_computation.36 | convolution fusion | flops 554958848 | bytes 19677216 | tf_op jit(solution)/shard_map/hqk,qhd->khd/dot_general | solution.py:396
  172.8 81.9 %all-gather.1 = bf16[32,1,1024]{2,1,0:T(2,128)(2,1)S(1)} all-gather(bf16[1,1,1024]{2,1,0:T(2,128)(2,1)S(1)} %convert_bitcast_fusion.1), channel_id=1, replica_groups=mesh['bucket'=32,'seq'=4] {'bucket'}, dimensions={0}, use_global_device_ids=true | all-gather | bytes 67584 | tf_op jit(solution)/shard_map/all_gather | solution.py:436
  254.8 2.0 convolution_convert_fusion.4
  256.8 9.0 %convolution_convert_fusion = bf16[4096,1024]{1,0:T(8,128)(2,1)} fusion(bf16[1,256,1024]{2,1,0:T(8,128)(2,1)S(1)} %copy-done.16, f32[1024]{0:T(1024)S(1)} %get-tuple-element.59, f32[256]{0:T(256)S(1)} %fusion.77, f32[256,4096]{1,0:T(8,128)} %copy-done.38, f32[4096]{0:T(1024)S(1)} %bitcast.164), kind=kOutput, calls=%fused_computation.19 | convolution fusion | flops 2163212288 | bytes 13128704 | tf_op jit(solution)/shard_map/dot_general | solution.py:264
  265.8 66.6 %reduce_fc2_proj.1 = (f32[2,16,1024]{2,1,0:T(8,128)}, f32[2,16,1024]{2,1,0:T(8,128)}, f32[2,16,1024]{2,1,0:T(8,128)}, f32[2,16,1024]{2,1,0:T(8,128)}, f32[2,16,1024]{2,1,0:T(8,128)}) custom-call(bf16[4,2,4,2,4,16,1024]{6,5,4,3,2,1,0:T(8,128)(2,1)} %bitcast.136, bf16[4,2,4,2,16,1024]{5,4,3,2,1,0:T(8,128)(2,1)} %bitcast.137), custom_call_target="tpu_custom_call" | custom-call | tf_op jit(solution)/shard_map/reduce_fc2_proj/pallas_call | solution.py:233
  332.4 1.1 pad_maximum_fusion.4
  333.5 0.8 copy.53
  334.4 38.2 %convert_reduce_fusion.5 = (f32[16,64]{1,0:T(8,128)S(1)}, bf16[16,64,256]{2,1,0:T(8,128)(2,1)}) fusion(bf16[1024,16,64]{0,2,1:T(8,128)(2,1)S(1)} %bitcast.139, f32[16,256,1024]{2,1,0:T(8,128)} %fusion.63, f32[16,256,1024]{2,1,0:T(8,128)} %copy-done.2, f32[16,256]{1,0:T(8,128)S(1)} %log_add_fusion, pred[256,1024]{1,0:T(8,128)(4,1)S(1)} %broadcast_compare_fusion), kind=kOutput, calls=%fused_computation.82 | convolution fusion | flops 583798784 | bytes 36458496 | tf_op jit(solution)/shard_map/hqk,khd->qhd/dot_general | solution.py:389
  372.7 7.4 %convolution_convert_fusion.1 = bf16[1024,4096]{1,0:T(8,128)(2,1)} fusion(bf16[256,4096]{1,0:T(8,128)(2,1)} %copy-done.10, f32[256,1024]{1,0:T(8,128)S(1)} %get-tuple-element.51, f32[1024]{0:T(1024)S(1)} %get-tuple-element.60, f32[1024]{0:T(1024)S(1)} %get-tuple-element.61, f32[256]{0:T(256)S(1)} %fusion.80, f32[256]{0:T(256)S(1)} %broadcast_multiply_fusion), kind=kOutput, calls=%fused_computation.20 | convolution fusion | flops 2152988672 | bytes 11544576 | tf_op jit(solution)/shard_map/dot_general | solution.py:264
  380.1 5.1 fusion.53
  385.2 0.6 fusion.51
  385.9 14.1 %psum.14 = bf16[6144]{0:T(1024)(128)(2,1)S(1)} all-reduce(f32[6144]{0:T(1024)S(1)} %constant_dynamic-update-slice_fusion.8), channel_id=1, replica_groups=mesh['bucket'=32,'seq'=4] {'seq'}, use_global_device_ids=true, to_apply=%region_19.20 | all-reduce | flops 6144 | bytes 36864 | tf_op jit(solution)/shard_map/psum | solution.py:433
  400.0 81.4 %all-gather = bf16[196608]{0:T(1024)(128)(2,1)S(1)} all-gather(bf16[6144]{0:T(1024)(128)(2,1)S(1)} %psum.14), channel_id=2, replica_groups=mesh['bucket'=32,'seq'=4] {'bucket'}, dimensions={0}, use_global_device_ids=true | all-gather | bytes 405504 | tf_op jit(solution)/shard_map/all_gather | solution.py:437
  481.5 0.2 convert_reduce_fusion.4
  481.7 62.9 %psum.15 = f32[8192]{0:T(1024)S(1)} all-reduce(f32[8192]{0:T(1024)S(1)} %constant_dynamic-update-slice_fusion.10), channel_id=1, replica_groups=mesh['bucket'=32,'seq'=4] {'bucket','seq'}, use_global_device_ids=true, to_apply=%region_26.27 | all-reduce | flops 8192 | bytes 65536 | tf_op jit(solution)/shard_map/psum | solution.py:443
  544.7 0.6 dynamic_slice.22
  545.2 0.6 dynamic_slice.20
  545.8 0.2 reshape.241
  546.1 1.2 fusion.69
  547.3 8.0 %fusion.114 = f32[1,1024]{1,0:T(1,128)S(1)} fusion(bf16[6144,1]{0,1:T(2,128)(2,1)S(1)} %reshape.247, bf16[1024,6144]{1,0:T(8,128)(2,1)} %param.23), kind=kOutput, calls=%fused_computation.170 | convolution fusion | flops 12582912 | bytes 12599296 | tf_op jit(solution)/shard_map/dot_general | solution.py:270
  555.4 1.5 add_bitcast_fusion
  556.8 4.8 convolution_convert_fusion.2
  561.6 87.8 %reduce_fc1_qkv.1 = (f32[2,16,1024]{2,1,0:T(8,128)}, f32[2,16,1024]{2,1,0:T(8,128)}, f32[2,16,1024]{2,1,0:T(8,128)}, f32[2,16,1024]{2,1,0:T(8,128)}, f32[2,16,10...) custom-call(bf16[4,2,4,2,16,4096]{5,4,3,2,1,0:T(8,128)(2,1)} %bitcast.135, ...), custom_call_target="tpu_custom_call" | custom-call | tf_op jit(solution)/shard_map/reduce_fc1_qkv/pallas_call | solution.py:233
  649.4 0.6 fusion.108
  650.0 0.6 dynamic_slice.19
  650.6 0.6 fusion.71
  651.3 1.8 pad_maximum_fusion.5
  653.1 1.9 pad_maximum_fusion.3
  655.0 0.7 copy.68
  (131 shorter events, 0.9 us)
Async XLA Ops:
  7.2 81.9 %copy-start = (bf16[1024,1024]{1,0:T(8,128)(2,1)S(1)}, bf16[1024,1024]{1,0:T(8,128)(2,1)}, u32[]{:S(2)}) copy-start(bf16[1024,1024]{1,0:T(8,128)(2,1)} %param.27) | copy-start | bytes 6291460
  7.2 6.6 copy-start.25
  7.2 6.6 copy-start.3
  7.2 40.8 %all-gather.7.cloned.1.call-start = ((), (), s32[]{:S(2)}) async-start(), calls=%async_computation.3 | async-start | bytes 2621440 | tf_op jit(solution)/shard_map/all_gather | solution.py:340
  7.3 7.0 %copy-start.32 = (bf16[1024,3072]{1,0:T(8,128)(2,1)S(1)}, bf16[1024,3072]{1,0:T(8,128)(2,1)}, u32[]{:S(2)}) copy-start(bf16[1024,3072]{1,0:T(8,128)(2,1)} %param.25) | copy-start | bytes 18874372
  14.3 4.6 copy-start.24
  16.2 1.7 copy-start.9
  17.9 3.9 copy-start.34
  17.9 3.9 copy-start.29
  17.9 4.8 copy-start.27
  17.9 4.8 copy-start.26
  17.9 4.8 copy-start.30
  17.9 4.8 copy-start.28
  17.9 7.5 %copy-start.35 = (s32[1,16]{1,0:T(1,128)S(1)}, s32[1,16]{1,0:T(1,128)}, u32[]{:S(2)}) copy-start(s32[1,16]{1,0:T(1,128)} %param.20) | copy-start | bytes 196
  18.8 57.6 %all-gather.5.cloned.1.call-start = ((), (), s32[]{:S(2)}) async-start(), calls=%async_computation.2 | async-start | bytes 2621440 | tf_op jit(solution)/shard_map/all_gather | solution.py:341
  21.5 358.6 %reduce-scatter.3.cloned.1.call-start = ((), (), s32[]{:S(2)}) async-start(), calls=%async_computation.4 | async-start | bytes 2621440 | tf_op jit(solution)/shard_map/reduce_scatter | solution.py:403
  22.6 33.8 %copy-start.11 = (bf16[256,1024]{0,1:T(8,128)(2,1)}, bf16[256,1024]{0,1:T(8,128)(2,1)S(1)}, u32[]{:S(2)}) copy-start(bf16[256,1024]{0,1:T(8,128)(2,1)S(1)} %copy.49) | copy-start | bytes 1572868
  56.5 6.2 copy-start.2
  80.3 10.0 %slice-start = ((s8[8388608]{0:T(1024)(128)(4,1)}), s8[4194304]{0:T(1024)(128)(4,1)S(1)}, s32[]{:S(2)}) async-start(s8[8388608]{0:T(1024)(128)(4,1)} %bitcast.167), calls=%async_computation.6 | async-start | bytes 8388608
  80.3 8.8 %copy-start.4 = (bf16[1,256,1024]{2,1,0:T(8,128)(2,1)S(1)}, bf16[1,256,1024]{2,1,0:T(8,128)(2,1)}, u32[]{:S(2)}) copy-start(bf16[1,256,1024]{2,1,0:T(8,128)(2,1)} %param.17) | copy-start | bytes 1572868
  80.3 10.0 %slice-start.1 = ((s8[8388608]{0:T(1024)(128)(4,1)}), s8[4194304]{0:T(1024)(128)(4,1)S(1)}, s32[]{:S(2)}) async-start(s8[8388608]{0:T(1024)(128)(4,1)} %bitcast.167), calls=%async_computation.7 | async-start | bytes 8388608
  89.1 3.8 copy-start.13
  89.1 3.8 slice-start.2
  90.3 2.6 copy-start.15
  90.3 2.8 slice-start.3
  92.9 6.6 copy-start.38
  99.4 2.9 copy-start.10
  102.8 7.0 %copy-start.7 = (f32[256,1024]{1,0:T(8,128)}, f32[256,1024]{1,0:T(8,128)S(1)}, u32[]{:S(2)}) copy-start(f32[256,1024]{1,0:T(8,128)S(1)} %get-tuple-element.49) | copy-start | bytes 3145732
  109.8 0.8 copy-start.20
  109.8 3.6 copy-start.31
  113.4 9.8 %copy-start.12 = (bf16[256,1024]{0,1:T(8,128)(2,1)S(1)}, bf16[256,1024]{0,1:T(8,128)(2,1)}, u32[]{:S(2)}) copy-start(bf16[256,1024]{0,1:T(8,128)(2,1)} %copy-done.11) | copy-start | bytes 1572868
  162.7 10.0 %copy-start.23 = (bf16[1,1024]{1,0:T(2,128)(2,1)S(1)}, bf16[1,1024]{1,0:T(2,128)(2,1)}, u32[]{:S(2)}) copy-start(bf16[1,1024]{1,0:T(2,128)(2,1)} %param.18) | copy-start | bytes 6148
  162.7 92.0 %copy-start.14 = (bf16[16,64,256]{2,1,0:T(8,128)(2,1)S(1)}, bf16[16,64,256]{2,1,0:T(8,128)(2,1)}, u32[]{:S(2)}) copy-start(bf16[16,64,256]{2,1,0:T(8,128)(2,1)} %copy-done.13) | copy-start | bytes 1572868
  162.7 92.0 %copy-start.21 = (bf16[256,1024]{1,0:T(8,128)(2,1)S(1)}, bf16[256,1024]{1,0:T(8,128)(2,1)}, u32[]{:S(2)}) copy-start(bf16[256,1024]{1,0:T(8,128)(2,1)} %copy-done.20) | copy-start | bytes 1572868
  162.7 217.4 %reduce-scatter.5.cloned.1.call-start = ((), (), s32[]{:S(2)}) async-start(), calls=%async_computation.5 | async-start | bytes 2621440 | tf_op jit(solution)/shard_map/reduce_scatter | solution.py:406
  172.7 84.1 %copy-start.16 = (bf16[1,256,1024]{2,1,0:T(8,128)(2,1)S(1)}, bf16[1,256,1024]{2,1,0:T(8,128)(2,1)}, u32[]{:S(2)}) copy-start(bf16[1,256,1024]{2,1,0:T(8,128)(2,1)} %param.33) | copy-start | bytes 1572868
  265.8 68.6 %copy-start.6 = (bf16[1024,1024]{0,1:T(8,128)(2,1)S(1)}, bf16[1024,1024]{0,1:T(8,128)(2,1)}, u32[]{:S(2)}) copy-start(bf16[1024,1024]{0,1:T(8,128)(2,1)} %copy.50) | copy-start | bytes 6291460
  372.7 7.4 %copy-start.5 = (bf16[1,256,1024]{2,1,0:T(8,128)(2,1)S(1)}, bf16[1,256,1024]{2,1,0:T(8,128)(2,1)}, u32[]{:S(2)}) copy-start(bf16[1,256,1024]{2,1,0:T(8,128)(2,1)} %param.17) | copy-start | bytes 1572868
  372.7 7.4 %copy-start.36 = (bf16[16,64,256]{2,1,0:T(8,128)(2,1)S(1)}, bf16[16,64,256]{2,1,0:T(8,128)(2,1)}, u32[]{:S(2)}) copy-start(bf16[16,64,256]{2,1,0:T(8,128)(2,1)} %get-tuple-element.78) | copy-start | bytes 1572868
  380.1 101.4 %copy-start.18 = (bf16[256,1024]{0,1:T(8,128)(2,1)S(1)}, bf16[256,1024]{0,1:T(8,128)(2,1)}, u32[]{:S(2)}) copy-start(bf16[256,1024]{0,1:T(8,128)(2,1)} %reduce-scatter.5.cloned.1.call-done) | copy-start | bytes 1572868
  547.3 8.1 %copy-start.8 = (f32[256,1024]{1,0:T(8,128)S(1)}, f32[256,1024]{1,0:T(8,128)}, u32[]{:S(2)}) copy-start(f32[256,1024]{1,0:T(8,128)} %copy-done.7) | copy-start | bytes 3145732
  547.3 8.1 %copy-start.17 = (bf16[1,256,1024]{2,1,0:T(8,128)(2,1)S(1)}, bf16[1,256,1024]{2,1,0:T(8,128)(2,1)}, u32[]{:S(2)}) copy-start(bf16[1,256,1024]{2,1,0:T(8,128)(2,1)} %param.33) | copy-start | bytes 1572868
  555.3 1.5 copy-start.19
  555.3 1.5 copy-start.33
  555.3 1.5 copy-start.37
  561.6 93.4 %copy-start.22 = (f32[2,16,1024]{2,1,0:T(8,128)S(1)}, f32[2,16,1024]{2,1,0:T(8,128)}, u32[]{:S(2)}) copy-start(f32[2,16,1024]{2,1,0:T(8,128)} %get-tuple-element.28) | copy-start | bytes 393220
  561.6 94.0 %copy-start.1 = (bf16[1024,1024]{1,0:T(8,128)(2,1)S(1)}, bf16[1024,1024]{1,0:T(8,128)(2,1)}, u32[]{:S(2)}) copy-start(bf16[1024,1024]{1,0:T(8,128)(2,1)} %param.27) | copy-start | bytes 6291460
Sparse Core Ops, SparseCore 0:
  18.9 29.0 all-gather.6
  50.3 26.0 all-gather.4
  162.8 38.0 reduce-scatter.2
  203.5 37.7 reduce-scatter.4
